TPU v7x, 512 devices: a whole 4x8x8 slice. The times are simulated.
512 devices in a mesh: dp: 16 (over z_hi, x, core), ctx: 32 (over y, z_lo).
Axes of the slice: x: 4, y: 8, z: 8 (z_hi: 2, z_lo: 4; z = z_hi * 4 + z_lo), core: 2. Of those that a mesh axis runs over, the one named last changes fastest.
Arguments:
- queries: bfloat16 [16, 16384, 512], P('dp', 'ctx'), may hold values from -36 to 36
- keys: bfloat16 [16, 16384, 512], P('dp', 'ctx'), may hold values from -36 to 36
- values: bfloat16 [16, 16384, 512], P('dp', 'ctx'), may hold values from -6 to 6
- grad_out: bfloat16 [16, 16384, 512], P('dp', 'ctx'), may hold values from -48 to 48
- gains: float32 [2, 512], replicated, may hold values from 0.1 to 1.9
Outputs:
- grad_queries: bfloat16 [16, 16384, 512], P('dp', 'ctx')
- grad_keys: bfloat16 [16, 16384, 512], P('dp', 'ctx')
- grad_values: bfloat16 [16, 16384, 512], P('dp', 'ctx')
- gain_grads: float32 [2, 512], P(None, 'dp')
All inputs are finite; a program needn't handle non-finite values.
Results may differ from a plain program's by a relative error of at most 0.0093.
Values may be sent and summed in bfloat16 or wider, within the bound.
A program may use at most 64 MiB of HBM per device.

v0:
```python
import math

import jax
import jax.numpy as jnp
from jax import lax
from jax.sharding import PartitionSpec as P

HEADS = 4
HD = 128
SPAN = 1


norm_eps = 1e-06


def from_behind(shard, axis, by):
    length = lax.axis_size(axis)
    pairs = [(i, i + by) for i in range(length) if 0 <= i + by < length]
    return lax.ppermute(shard, axis, pairs)


def unit_rows(inputs, heads):
    count = inputs.shape[0]
    wide = inputs.astype(jnp.float32).reshape(count, heads, -1)
    inverse = lax.rsqrt(jnp.mean(wide * wide, axis=2, keepdims=True) + norm_eps)
    return (wide * inverse, inverse)


def norm_backward(grad_norm, unit, inverse, gain):
    count, heads, head_dim = unit.shape
    grad_three = grad_norm.reshape(count, heads, head_dim)
    scaled = grad_three * gain
    mean_term = jnp.mean(scaled * unit, axis=2, keepdims=True)
    grad_in = inverse * (scaled - unit * mean_term)
    gain_grad = jnp.sum(grad_three * unit, axis=0).reshape(-1)
    return (grad_in.reshape(count, -1).astype(jnp.bfloat16), gain_grad)


def cross(left, right):
    return jnp.einsum("ad,cd->ac", left, right, preferred_element_type=jnp.float32)


def inner(left, right):
    return jnp.einsum("ac,ad->cd", left, right, preferred_element_type=jnp.float32)


def per_device(queries, keys, values, grad_out, gains):
    heads = HEADS
    head_dim = HD
    span = SPAN
    rows = queries.shape[1]
    reach = span * rows
    scale = 1.0 / math.sqrt(head_dim)
    place = lax.axis_index("ctx")
    q_unit, q_inv = unit_rows(queries[0], heads)
    k_unit, k_inv = unit_rows(keys[0], heads)
    q_gain = gains[0].reshape(heads, head_dim)
    k_gain = gains[1].reshape(heads, head_dim)
    q_norm = (q_unit * q_gain).reshape(rows, -1).astype(jnp.bfloat16)
    k_norm = (k_unit * k_gain).reshape(rows, -1).astype(jnp.bfloat16)
    upstream = grad_out[0]
    own = jnp.stack([k_norm, values[0]])
    tiles = [own]
    step = 1
    tiles.append(from_behind(own, "ctx", step))
    window = jnp.concatenate(tiles[::-1], axis=1)
    query_pos = lax.broadcasted_iota(jnp.int32, (rows, (span + 1) * rows), 0)
    key_pos = lax.broadcasted_iota(jnp.int32, (rows, (span + 1) * rows), 1)
    visible = (
        (key_pos > query_pos) & (key_pos <= query_pos + reach) & (key_pos >= (span - place) * rows)
    )
    first_key = 0
    dq_parts, dk_parts, dv_parts, lse_parts, delta_parts = ([], [], [], [], [])
    for head in range(heads):
        cols = slice(head * head_dim, (head + 1) * head_dim)
        q_head = q_norm[:, cols]
        k_head = window[0, :, cols]
        v_head = window[1, :, cols]
        g_head = upstream[:, cols]
        scores = cross(q_head, k_head) * scale
        total = jnp.sum(jnp.where(visible, jnp.exp(scores), 0.0), axis=1, keepdims=True)
        log_total = jnp.log(total)
        probs = jnp.where(visible, jnp.exp(scores - log_total), 0.0)
        probs_low = probs.astype(jnp.bfloat16)
        attended = jnp.dot(probs_low, v_head, preferred_element_type=jnp.float32)
        delta = jnp.sum(g_head.astype(jnp.float32) * attended, axis=1, keepdims=True)
        grad_scores = (probs * (cross(g_head, v_head) - delta)).astype(jnp.bfloat16)
        dq_parts.append(jnp.dot(grad_scores, k_head, preferred_element_type=jnp.float32) * scale)
        dk_parts.append(inner(grad_scores, q_head) * scale)
        dv_parts.append(inner(probs_low, g_head))
        lse_parts.append(log_total[:, 0])
        delta_parts.append(delta[:, 0])
    grad_qn = jnp.concatenate(dq_parts, axis=1)
    key_grads = jnp.stack([jnp.concatenate(dk_parts, axis=1), jnp.concatenate(dv_parts, axis=1)])
    local = key_grads[:, span * rows :]
    step = 1
    term = key_grads[:, (span - step) * rows : (span - step + 1) * rows]
    local = local + from_behind(term, "ctx", -step)
    grad_queries, q_gain_grad = norm_backward(grad_qn, q_unit, q_inv, q_gain)
    grad_keys, k_gain_grad = norm_backward(local[0], k_unit, k_inv, k_gain)
    grad_values = local[1].astype(jnp.bfloat16)
    gain_terms = jnp.stack([q_gain_grad, k_gain_grad])
    gain_total = lax.psum(gain_terms, "ctx")
    gain_share = lax.psum_scatter(gain_total, "dp", scatter_dimension=1, tiled=True)
    return (grad_queries[None], grad_keys[None], grad_values[None], gain_share)


def solution(mesh):
    placed = (
        P("dp", "ctx", None),
        P("dp", "ctx", None),
        P("dp", "ctx", None),
        P("dp", "ctx", None),
        P(),
    )
    return jax.shard_map(
        per_device,
        mesh=mesh,
        in_specs=placed,
        out_specs=(P("dp", "ctx", None), P("dp", "ctx", None), P("dp", "ctx", None), P(None, "dp")),
        check_vma=False,
    )
```

profile of v0, /device:TPU:2, one launch (start us, length us, event | category | flops | bytes accessed | tf_op | source)
XLA Modules:
  0.0 287.6 jit_solution(17089914442977109020)
XLA Ops:
  8.0 1.3 copy.21
  9.2 1.3 copy.22
  10.5 1.2 multiply_reduce_fusion.3
  11.8 1.1 pad_maximum_fusion.1
  13.0 5.3 %collective-permute-start = (bf16[2,512,512]{1,2,0:T(8,128)(2,1)}, bf16[2,512,512]{1,2,0:T(8,128)(2,1)}, u32[]{:S(2)}, u32[]{:S(2)}) collective-permute-start(bf16[2,512,512]{1,2,0:T(8,128)(2,1)} %pad_maximum_fusion.1), channel_id=1, source_target_pairs={{0,1},{1,2},{2,3},{3,4},{4,5},{5,6},{6,7},{7,8},{8,9},{9,10},{10,1... | collective-permute-start | bytes 3145736 | tf_op jit(solution)/shard_map/ppermute | solution.py:19
  18.4 1.3 copy.23
  20.1 19.8 %collective-permute-done = bf16[2,512,512]{1,2,0:T(8,128)(2,1)} collective-permute-done((bf16[2,512,512]{1,2,0:T(8,128)(2,1)}, bf16[2,512,512]{1,2,0:T(8,128)(2,1)}, u32[]{:S(2)}, u32[]{:S(2)}) %collective-permute-start) | collective-permute-done | bytes 1048608 | tf_op jit(solution)/shard_map/ppermute | solution.py:19
  40.0 1.5 maximum_maximum_fusion
  42.9 2.0 select_reduce_fusion.3
  44.9 2.4 fusion.8
  50.6 1.0 fusion.5
  51.6 1.0 fusion.3
  52.7 1.0 fusion.4
  53.7 1.0 fusion.2
  56.8 1.5 collective-permute-start.1
  61.0 44.9 %collective-permute-done.1 = f32[2,512,512]{1,2,0:T(8,128)S(1)} collective-permute-done((f32[2,512,512]{1,2,0:T(8,128)S(1)}, f32[2,512,512]{1,2,0:T(8,128)S(1)}, u32[]{:S(2)}, u32[]{:S(2)}) %collective-permute-start.1) | collective-permute-done | bytes 2097184 | tf_op jit(solution)/shard_map/ppermute | solution.py:19
  106.5 1.1 copy-done
  107.9 1.1 multiply_reduce_fusion
  109.0 0.9 copy.35
  109.9 1.0 copy.28
  111.0 1.0 copy.30
  112.0 1.0 copy.29
  113.0 88.8 %reduce-scatter.4.cloned.1.call-done = f32[32,2]{1,0:T(8,128)} async-done(((f32[512,2]{1,0:T(8,128)}), f32[32,2]{1,0:T(8,128)}) %reduce-scatter.4.cloned.1.call-update) | async-done | bytes 272
  202.5 78.3 %psum.8 = f32[2,32]{1,0:T(2,128)} all-reduce(f32[2,32]{1,0:T(2,128)S(1)} %copy.36), channel_id=1, replica_groups=mesh['dp'=16,'ctx'=32] {'ctx'}, use_global_device_ids=true, to_apply=%region_14.15 | all-reduce | flops 64 | bytes 512 | tf_op jit(solution)/shard_map/psum | solution.py:103
  (52 shorter events, 12.6 us)
Async XLA Ops:
  7.2 194.6 %reduce-scatter.4.cloned.1.call-start = ((), (), s32[]{:S(2)}) async-start(), calls=%async_computation.1 | async-start | bytes 278528
  10.5 7.7 %copy-start.2 = (bf16[1,512,512]{2,1,0:T(8,128)(2,1)S(1)}, bf16[1,512,512]{2,1,0:T(8,128)(2,1)}, u32[]{:S(2)}) copy-start(bf16[1,512,512]{2,1,0:T(8,128)(2,1)} %param.5) | copy-start | bytes 1572868
  13.0 27.0 %collective-permute-start = (bf16[2,512,512]{1,2,0:T(8,128)(2,1)}, bf16[2,512,512]{1,2,0:T(8,128)(2,1)}, u32[]{:S(2)}, u32[]{:S(2)}) collective-permute-start(bf16[2,512,512]{1,2,0:T(8,128)(2,1)} %pad_maximum_fusion.1), channel_id=1, source_target_pairs={{0,1},{1,2},{2,3},{3,4},{4,5},{5,6},{6,7},{7,8},{8,9},{9,10},{10,1... | collective-permute-start | bytes 3145736 | tf_op jit(solution)/shard_map/ppermute | solution.py:19
  56.8 49.1 %collective-permute-start.1 = (f32[2,512,512]{1,2,0:T(8,128)S(1)}, f32[2,512,512]{1,2,0:T(8,128)S(1)}, u32[]{:S(2)}, u32[]{:S(2)}) collective-permute-start(f32[2,512,512]{1,2,0:T(8,128)S(1)} %pad_maximum_fusion), channel_id=1, source_target_pairs={{1,0},{2,1},{3,2},{4,3},{5,4},{6,5},{7,6},{8,7},{9,8},{10,9},{11,1... | collective-permute-start | bytes 6291464 | tf_op jit(solution)/shard_map/ppermute | solution.py:19
  106.4 1.2 copy-start
  110.9 1.1 copy-start.1
Sparse Core Ops, SparseCore 0:
  110.0 91.6 reduce-scatter.3
where the time goes:
time: 288 us
  waiting for transfers between devices  154 us (53%)
  blocking collectives  78.3 us (27%)
  between operations  14.4 us (5%)
  matrix products  13.8 us (5%)
  local copies, waits for them, and re-layouts  10.7 us (4%)
  other arithmetic  10.2 us (4%)
  starting transfers between devices  6.81 us (2%)
    unnamed x2, waiting for transfers between devices  88.8 us
    psum x1, blocking collectives, per_device(): gain_total = lax.psum(gain_terms, 'ctx')  78.3 us
    ppermute x2, waiting for transfers between devices, from_behind(): return lax.ppermute(shard, axis, pairs)  64.8 us
    unnamed x15, local copies, waits for them, and re-layouts  9.78 us
    dot_general x8, matrix products, cross(): jnp.einsum('ad,cd->ac', left, right, preferred_element_type=jnp.float32)  7.34 us
    ppermute x2, starting transfers between devices, from_behind(): return lax.ppermute(shard, axis, pairs)  6.77 us
  transfers between devices with their start and end apart: 3, of which 3 were waited for; matrix products, arithmetic and copies ran while one was open for 3% of the time, Pallas kernels for 0%

commit v1 on v0

v1 whole, which is shorter than its diff:
```python
import functools
import math

import jax
import jax.numpy as jnp
from jax import lax
from jax.experimental import pallas as pl
from jax.experimental.pallas import tpu as pltpu
from jax.sharding import PartitionSpec as P

HEADS = 4
HD = 128
EPS = 1e-06
HALF = 256
SCALE = 1.0 / math.sqrt(HD)
EXP2_SCALE = SCALE * math.log2(math.e)
MESH = pl.DeviceIdType.MESH

OWN_BLOCKS = ((0, 0, True), (0, 1, False), (1, 1, True))
AHEAD_BLOCKS = ((0, 0, True), (1, 0, False), (1, 1, True))


def half(i):
    return pl.ds(i * HALF, HALF)


def dot_nt(a, b):
    return lax.dot_general(a, b, (((1,), (1,)), ((), ())), preferred_element_type=jnp.float32)


def dot(a, b):
    return jnp.dot(a, b, preferred_element_type=jnp.float32)


def unit_rows(x):
    wide = x.astype(jnp.float32)
    inverse = lax.rsqrt(jnp.mean(wide * wide, axis=1, keepdims=True) + EPS)
    return wide * inverse, inverse


def norm_back(grad, unit, inverse, gain):
    scaled = grad * gain
    mean_term = jnp.mean(scaled * unit, axis=1, keepdims=True)
    return (inverse * (scaled - unit * mean_term)).astype(jnp.bfloat16)


def exps_and_sums(h, blocks, own, kn, v, qn, g, qh, e, gp, eh, sums):
    total = [None, None]
    weighted = [None, None]
    for kb, qb, edge in blocks:
        s = dot_nt(kn[h, half(kb), :], qn[qh, half(qb), :])
        ex = jnp.exp2(s * EXP2_SCALE)
        if edge:
            key = lax.broadcasted_iota(jnp.int32, (HALF, HALF), 0)
            query = lax.broadcasted_iota(jnp.int32, (HALF, HALF), 1)
            ex = jnp.where(key <= query if own else key > query, ex, 0.0)
        gr = dot_nt(v[h, half(kb), :], g[h, half(qb), :])
        e[eh, half(kb), half(qb)] = ex
        gp[eh, half(kb), half(qb)] = gr
        t = jnp.sum(ex, axis=0, keepdims=True)
        w = jnp.sum(ex * gr, axis=0, keepdims=True)
        total[qb] = t if total[qb] is None else total[qb] + t
        weighted[qb] = w if weighted[qb] is None else weighted[qb] + w
    for qb in range(2):
        for i in range(2):
            sums[h, pl.ds(2 * qb + i, 1), :] = total[qb][:, i * HD : (i + 1) * HD]
            sums[h, pl.ds(4 + 2 * qb + i, 1), :] = weighted[qb][:, i * HD : (i + 1) * HD]


def row_pair(ref, h, first):
    return jnp.concatenate([ref[h, pl.ds(first, 1), :], ref[h, pl.ds(first + 1, 1), :]], axis=1)


def probs_and_grads(h, blocks, e, gp, eh, sums_a, sums_b, keep, p_low, ds_low):
    recip, delta = [], []
    for qb in range(2):
        r = 1.0 / (row_pair(sums_a, h, 2 * qb) + row_pair(sums_b, h, 2 * qb))
        delta.append((row_pair(sums_a, h, 4 + 2 * qb) + row_pair(sums_b, h, 4 + 2 * qb)) * r)
        recip.append(r if keep is None else r * keep)
    for kb, qb, _ in blocks:
        p = e[eh, half(kb), half(qb)] * recip[qb]
        p_low[half(kb), half(qb)] = p.astype(jnp.bfloat16)
        ds_low[half(kb), half(qb)] = (p * (gp[eh, half(kb), half(qb)] - delta[qb])).astype(jnp.bfloat16)


def kernel(
    n_dp, n_ctx,
    q_hbm, k_hbm, v_hbm, g_hbm, gains,
    dq_hbm, dk_hbm, dv_hbm, gain_out,
    q, k, v, g, rq, rg, qn, kn, kt, rqn,
    e_own, gp_own, e_ahead, gp_ahead, p_low, ds_low,
    dk_acc, dv_acc, dq_own, dq_give, dq_take, dq_o, dk_o, dv_o,
    own_sums, right_sums, ahead_sums, left_sums,
    gain_part, dp_terms, ctx_terms,
    load_sem, fwd_send, fwd_recv, own_send, own_recv, ahead_send, ahead_recv,
    dq_send, dq_recv, out_sem, dp_send, dp_recv, ctx_send, ctx_recv,
):
    me_d, me_c = lax.axis_index("dp"), lax.axis_index("ctx")
    left, right = lax.rem(me_c + n_ctx - 1, n_ctx), lax.rem(me_c + 1, n_ctx)
    width = HEADS * HD // n_dp
    has_ahead = jnp.where(me_c < n_ctx - 1, 1.0, 0.0).astype(jnp.float32)

    loads = ((q_hbm, q), (g_hbm, g), (k_hbm, k), (v_hbm, v))

    def load(a, h):
        src, dst = loads[a]
        return pltpu.make_async_copy(src.at[0, :, pl.ds(h * HD, HD)], dst.at[h], load_sem.at[a, h])

    for h in range(HEADS):
        for a in range(4):
            load(a, h).start()

    barrier = pltpu.get_barrier_semaphore()

    @pl.loop(1, n_dp)
    def _(i):
        pl.semaphore_signal(barrier, inc=1, device_id={"dp": lax.rem(me_d + i, n_dp)}, device_id_type=MESH)

    @pl.loop(1, n_ctx)
    def _(i):
        pl.semaphore_signal(barrier, inc=1, device_id={"ctx": lax.rem(me_c + i, n_ctx)}, device_id_type=MESH)

    pl.semaphore_wait(barrier, n_dp + n_ctx - 2)

    def to_left(src, dst, send, recv):
        return pltpu.make_async_remote_copy(src, dst, send, recv, device_id={"ctx": left}, device_id_type=MESH)

    def to_right(src, dst, send, recv):
        return pltpu.make_async_remote_copy(src, dst, send, recv, device_id={"ctx": right}, device_id_type=MESH)

    def send_q(h):
        return to_left(q.at[h], rq.at[h], fwd_send.at[0, h], fwd_recv.at[0, h])

    def send_g(h):
        return to_left(g.at[h], rg.at[h], fwd_send.at[1, h], fwd_recv.at[1, h])

    def send_own_sums(h):
        return to_left(own_sums.at[h], right_sums.at[h], own_send.at[h], own_recv.at[h])

    def send_ahead_sums(h):
        return to_right(ahead_sums.at[h], left_sums.at[h], ahead_send.at[h], ahead_recv.at[h])

    def send_dq(h):
        return to_right(dq_give.at[h], dq_take.at[h], dq_send.at[h], dq_recv.at[h])

    def store(a, h):
        src, dst = ((dq_o, dq_hbm), (dk_o, dk_hbm), (dv_o, dv_hbm))[a]
        cols = pl.ds(pl.multiple_of(h * HD, HD), HD)
        return pltpu.make_async_copy(src.at[h], dst.at[0, :, cols], out_sem.at[a, h])

    for h in range(HEADS):
        load(0, h).wait()
        load(1, h).wait()
        send_q(h).start()
        send_g(h).start()
    for h in range(HEADS):
        load(2, h).wait()
        load(3, h).wait()

    def gain_row(row, h):
        return gains[pl.ds(row, 1), pl.ds(pl.multiple_of(h * HD, HD), HD)]

    @pl.loop(0, HEADS)
    def _(h):
        for i in range(2):
            unit_q, _ = unit_rows(q[h, half(i), :])
            qn[h, half(i), :] = (unit_q * gain_row(0, h)).astype(jnp.bfloat16)
            unit_k, _ = unit_rows(k[h, half(i), :])
            normed = unit_k * gain_row(1, h)
            kn[h, half(i), :] = normed.astype(jnp.bfloat16)
            kt[h, :, half(i)] = normed.T.astype(jnp.bfloat16)
        exps_and_sums(h, OWN_BLOCKS, True, kn, v, qn, g, h, e_own, gp_own, h, own_sums)
        send_own_sums(h).start()

    def finish_dq(h):
        send_dq(h).wait_recv()
        for i in range(2):
            grad = dq_own[h, half(i), :] + dq_take[h, half(i), :].astype(jnp.float32)
            unit_q, inv_q = unit_rows(q[h, half(i), :])
            dq_o[h, half(i), :] = norm_back(grad, unit_q, inv_q, gain_row(0, h))
        store(0, h).start()

    @pl.loop(0, HEADS)
    def _(h):
        send_q(h).wait_recv()
        for i in range(2):
            unit_q, _ = unit_rows(rq[h, half(i), :])
            rqn[0, half(i), :] = (unit_q * gain_row(0, h)).astype(jnp.bfloat16)
        send_g(h).wait_recv()
        exps_and_sums(h, AHEAD_BLOCKS, False, kn, v, rqn, rg, 0, e_ahead, gp_ahead, 0, ahead_sums)
        ahead_sums[h] = ahead_sums[h] * has_ahead
        send_ahead_sums(h).start()
        send_own_sums(h).wait_recv()
        probs_and_grads(h, AHEAD_BLOCKS, e_ahead, gp_ahead, 0, right_sums, ahead_sums, has_ahead, p_low, ds_low)
        gain_q = jnp.zeros((1, HD), jnp.float32)
        for i in range(2):
            if i == 0:
                dqt = dot(kt[h], ds_low[:, half(0)])
            else:
                dqt = dot(kt[h, :, half(1)], ds_low[half(1), half(1)])
            grad = dqt.T * SCALE
            dq_give[h, half(i), :] = grad.astype(jnp.bfloat16)
            unit_q, _ = unit_rows(rq[h, half(i), :])
            gain_q += jnp.sum(grad * unit_q, axis=0, keepdims=True)
        send_dq(h).start()
        dk_acc[half(0), :] = dot(ds_low[half(0), half(0)], rqn[0, half(0), :])
        dk_acc[half(1), :] = dot(ds_low[half(1), :], rqn[0])
        dv_acc[half(0), :] = dot(p_low[half(0), half(0)], rg[h, half(0), :])
        dv_acc[half(1), :] = dot(p_low[half(1), :], rg[h])

        send_ahead_sums(h).wait_recv()
        probs_and_grads(h, OWN_BLOCKS, e_own, gp_own, h, own_sums, left_sums, None, p_low, ds_low)
        gain_k = jnp.zeros((1, HD), jnp.float32)
        for i in range(2):
            if i == 0:
                dk = dot(ds_low[half(0), :], qn[h])
                dv = dot(p_low[half(0), :], g[h])
                dqt = dot(kt[h, :, half(0)], ds_low[half(0), half(0)])
            else:
                dk = dot(ds_low[half(1), half(1)], qn[h, half(1), :])
                dv = dot(p_low[half(1), half(1)], g[h, half(1), :])
                dqt = dot(kt[h], ds_low[:, half(1)])
            dv_o[h, half(i), :] = (dv + dv_acc[half(i), :]).astype(jnp.bfloat16)
            grad_k = (dk + dk_acc[half(i), :]) * SCALE
            unit_k, inv_k = unit_rows(k[h, half(i), :])
            gain_k += jnp.sum(grad_k * unit_k, axis=0, keepdims=True)
            dk_o[h, half(i), :] = norm_back(grad_k, unit_k, inv_k, gain_row(1, h))
            grad_q = dqt.T * SCALE
            unit_q, _ = unit_rows(q[h, half(i), :])
            gain_q += jnp.sum(grad_q * unit_q, axis=0, keepdims=True)
            dq_own[h, half(i), :] = grad_q
        gain_part[h, pl.ds(0, 1), :] = gain_q
        gain_part[h, pl.ds(1, 1), :] = gain_k
        store(1, h).start()
        store(2, h).start()

        @pl.when(h > 0)
        def _():
            finish_dq(h - 1)

    def head_of(d):
        return lax.div(d * width, HD)

    def send_dp(i):
        to = lax.rem(me_d + i, n_dp)
        return pltpu.make_async_remote_copy(
            gain_part.at[head_of(to)], dp_terms.at[i], dp_send.at[i], dp_recv.at[i],
            device_id={"dp": to}, device_id_type=MESH,
        )

    def send_ctx(i):
        to = lax.rem(me_c + i, n_ctx)
        return pltpu.make_async_remote_copy(
            ctx_terms.at[me_c], ctx_terms.at[me_c], ctx_send.at[i], ctx_recv.at[i],
            device_id={"ctx": to}, device_id_type=MESH,
        )

    @pl.loop(1, n_dp)
    def _(i):
        send_dp(i).start()

    @pl.loop(1, n_dp)
    def _(i):
        send_dp(i).wait_recv()

    term = gain_part[head_of(me_d)]
    for i in range(1, n_dp):
        term = term + dp_terms[i]
    ctx_terms[me_c] = term

    @pl.loop(1, n_ctx)
    def _(i):
        send_ctx(i).start()

    finish_dq(HEADS - 1)

    def from_ctx(i):
        at = lax.rem(me_c + n_ctx - i, n_ctx)
        return pltpu.make_async_remote_copy(
            ctx_terms.at[at], ctx_terms.at[at], ctx_send.at[i], ctx_recv.at[i],
            device_id={"ctx": lax.rem(me_c + i, n_ctx)}, device_id_type=MESH,
        )

    @pl.loop(1, n_ctx)
    def _(i):
        from_ctx(i).wait_recv()

    total = ctx_terms[0]
    for i in range(1, n_ctx):
        total = total + ctx_terms[i]
    per_head = HD // width
    for j in range(per_head):

        @pl.when(lax.rem(me_d, per_head) == j)
        def _(j=j):
            gain_out[...] = total[:, j * width : (j + 1) * width]

    @pl.loop(0, HEADS)
    def _(h):
        send_q(h).wait_send()
        send_g(h).wait_send()
        send_own_sums(h).wait_send()
        send_ahead_sums(h).wait_send()
        send_dq(h).wait_send()
        for a in range(3):
            store(a, h).wait()

    @pl.loop(1, n_dp)
    def _(i):
        send_dp(i).wait_send()

    @pl.loop(1, n_ctx)
    def _(i):
        send_ctx(i).wait_send()


def per_device(n_dp, n_ctx, queries, keys, values, grad_out, gains):
    rows = queries.shape[1]
    low, wide = jnp.bfloat16, jnp.float32
    heads_low = pltpu.VMEM((HEADS, rows, HD), low)
    sums = pltpu.VMEM((HEADS, 8, HD), wide)
    dma = pltpu.SemaphoreType.DMA
    any_space = pl.BlockSpec(memory_space=pl.ANY)
    vmem = pl.BlockSpec(memory_space=pltpu.VMEM)
    big = jax.ShapeDtypeStruct(queries.shape, low)
    return pl.pallas_call(
        functools.partial(kernel, n_dp, n_ctx),
        out_shape=(big, big, big, jax.ShapeDtypeStruct((2, HEADS * HD // n_dp), wide)),
        in_specs=[any_space] * 4 + [vmem],
        out_specs=(any_space, any_space, any_space, vmem),
        scratch_shapes=[heads_low] * 8
        + [
            pltpu.VMEM((HEADS, HD, rows), low),
            pltpu.VMEM((1, rows, HD), low),
            pltpu.VMEM((HEADS, rows, rows), wide),
            pltpu.VMEM((HEADS, rows, rows), wide),
            pltpu.VMEM((1, rows, rows), wide),
            pltpu.VMEM((1, rows, rows), wide),
            pltpu.VMEM((rows, rows), low),
            pltpu.VMEM((rows, rows), low),
            pltpu.VMEM((rows, HD), wide),
            pltpu.VMEM((rows, HD), wide),
            pltpu.VMEM((HEADS, rows, HD), wide),
        ]
        + [heads_low] * 5
        + [sums] * 4
        + [
            pltpu.VMEM((HEADS, 2, HD), wide),
            pltpu.VMEM((n_dp, 2, HD), wide),
            pltpu.VMEM((n_ctx, 2, HD), wide),
            dma((4, HEADS)),
            dma((2, HEADS)),
            dma((2, HEADS)),
            dma((HEADS,)),
            dma((HEADS,)),
            dma((HEADS,)),
            dma((HEADS,)),
            dma((HEADS,)),
            dma((HEADS,)),
            dma((3, HEADS)),
            dma((n_dp,)),
            dma((n_dp,)),
            dma((n_ctx,)),
            dma((n_ctx,)),
        ],
        compiler_params=pltpu.CompilerParams(
            collective_id=0, has_side_effects=True, vmem_limit_bytes=48 * 1024 * 1024
        ),
    )(queries, keys, values, grad_out, gains)


def solution(mesh):
    placed = (
        P("dp", "ctx", None),
        P("dp", "ctx", None),
        P("dp", "ctx", None),
        P("dp", "ctx", None),
        P(),
    )
    return jax.shard_map(
        functools.partial(per_device, mesh.shape["dp"], mesh.shape["ctx"]),
        mesh=mesh,
        in_specs=placed,
        out_specs=(P("dp", "ctx", None), P("dp", "ctx", None), P("dp", "ctx", None), P(None, "dp")),
        check_vma=False,
    )
```

time: 288 us -> 80.8 us (0.28)
  the two profiles are of different devices: /device:TPU:2 before, /device:TPU:1 now
where the time goes in v1:
time: 80.8 us; the launch traced here: 80.5 us
  Pallas kernels  72 us (89%)
  local copies, waits for them, and re-layouts  7.79 us (10%)
    pallas_call x1, Pallas kernels, per_device(): pl.pallas_call(functools.partial(kernel, n_dp, n_ctx), out_shape=(big, bi...  72 us
    unnamed x14, local copies, waits for them, and re-layouts  7.79 us

profile of v1, /device:TPU:1, one launch (start us, length us, event | category | flops | bytes accessed | tf_op | source)
XLA Modules:
  0.0 80.5 jit_solution(10986228810244975127)
XLA Ops:
  0.6 0.0 copy-start
  0.6 1.0 %copy-done = bf16[1,512,512]{2,1,0:T(8,128)(2,1)S(1)} copy-done((bf16[1,512,512]{2,1,0:T(8,128)(2,1)S(1)}, bf16[1,512,512]{2,1,0:T(8,128)(2,1)}, u32[]{:S(2)}) %copy-start) | copy-done | bytes 524312
  1.7 0.0 copy-start.1
  1.7 1.0 %copy-done.1 = bf16[1,512,512]{2,1,0:T(8,128)(2,1)S(1)} copy-done((bf16[1,512,512]{2,1,0:T(8,128)(2,1)S(1)}, bf16[1,512,512]{2,1,0:T(8,128)(2,1)}, u32[]{:S(2)}) %copy-start.1) | copy-done | bytes 524312
  2.7 0.0 copy-start.2
  2.7 1.0 %copy-done.2 = bf16[1,512,512]{2,1,0:T(8,128)(2,1)S(1)} copy-done((bf16[1,512,512]{2,1,0:T(8,128)(2,1)S(1)}, bf16[1,512,512]{2,1,0:T(8,128)(2,1)}, u32[]{:S(2)}) %copy-start.2) | copy-done | bytes 524312
  3.8 0.0 copy-start.3
  3.8 1.0 %copy-done.3 = bf16[1,512,512]{2,1,0:T(8,128)(2,1)S(1)} copy-done((bf16[1,512,512]{2,1,0:T(8,128)(2,1)S(1)}, bf16[1,512,512]{2,1,0:T(8,128)(2,1)}, u32[]{:S(2)}) %copy-start.3) | copy-done | bytes 524312
  4.8 0.0 copy-start.4
  4.8 0.7 copy-done.4
  5.5 72.0 %shard_map.84 = (bf16[1,512,512]{2,1,0:T(8,128)(2,1)S(1)}, bf16[1,512,512]{2,1,0:T(8,128)(2,1)S(1)}, bf16[1,512,512]{2,1,0:T(8,128)(2,1)S(1)}, f32[2,32]{1,0:T(2,128)S(1)}) custom-call(bf16[1,512,512]{2,1,0:T(8,128)(2,1)S(1)} %copy-done, bf16[1,512,512]{2,1,0:T(8,128)(2,1)S(1)} %copy-done.1, bf16[1,512,512]{2,1,0:T(8,128)(2,1)S(1)} %copy-done.2, ...), custom_call_target="tpu_custom_call" | custom-call | tf_op jit(solution)/shard_map/pallas_call | solution.py:326
  77.5 0.8 copy.13
  78.3 0.8 copy.14
  79.1 0.8 copy.15
  79.9 0.6 copy.16
Async XLA Ops:
  0.6 1.0 %copy-start = (bf16[1,512,512]{2,1,0:T(8,128)(2,1)S(1)}, bf16[1,512,512]{2,1,0:T(8,128)(2,1)}, u32[]{:S(2)}) copy-start(bf16[1,512,512]{2,1,0:T(8,128)(2,1)} %q_hbm.1) | copy-start | bytes 1572868
  1.7 1.0 %copy-start.1 = (bf16[1,512,512]{2,1,0:T(8,128)(2,1)S(1)}, bf16[1,512,512]{2,1,0:T(8,128)(2,1)}, u32[]{:S(2)}) copy-start(bf16[1,512,512]{2,1,0:T(8,128)(2,1)} %k_hbm.1) | copy-start | bytes 1572868
  2.7 1.0 %copy-start.2 = (bf16[1,512,512]{2,1,0:T(8,128)(2,1)S(1)}, bf16[1,512,512]{2,1,0:T(8,128)(2,1)}, u32[]{:S(2)}) copy-start(bf16[1,512,512]{2,1,0:T(8,128)(2,1)} %v_hbm.1) | copy-start | bytes 1572868
  3.8 1.0 %copy-start.3 = (bf16[1,512,512]{2,1,0:T(8,128)(2,1)S(1)}, bf16[1,512,512]{2,1,0:T(8,128)(2,1)}, u32[]{:S(2)}) copy-start(bf16[1,512,512]{2,1,0:T(8,128)(2,1)} %g_hbm.1) | copy-start | bytes 1572868
  4.8 0.7 copy-start.4

commit v2 on v1

--- a/solution.py
+++ b/solution.py
@@ -148,11 +148,15 @@
         cols = pl.ds(pl.multiple_of(h * HD, HD), HD)
         return pltpu.make_async_copy(src.at[h], dst.at[0, :, cols], out_sem.at[a, h])
 
+    def send_ahead(h):
+        send_q(h).start()
+        send_g(h).start()
+
     for h in range(HEADS):
         load(0, h).wait()
         load(1, h).wait()
-        send_q(h).start()
-        send_g(h).start()
+        if h == 0:
+            send_ahead(0)
     for h in range(HEADS):
         load(2, h).wait()
         load(3, h).wait()
@@ -172,6 +176,13 @@
         exps_and_sums(h, OWN_BLOCKS, True, kn, v, qn, g, h, e_own, gp_own, h, own_sums)
         send_own_sums(h).start()
 
+        @pl.when(h == 1)
+        def _():
+            send_ahead(1)
+
+    send_ahead(2)
+    send_ahead(3)
+
     def finish_dq(h):
         send_dq(h).wait_recv()
         for i in range(2):
@@ -187,6 +198,11 @@
             unit_q, _ = unit_rows(rq[h, half(i), :])
             rqn[0, half(i), :] = (unit_q * gain_row(0, h)).astype(jnp.bfloat16)
         send_g(h).wait_recv()
+
+        @pl.when(h == HEADS - 1)
+        def _():
+            send_dq(0).start()
+
         exps_and_sums(h, AHEAD_BLOCKS, False, kn, v, rqn, rg, 0, e_ahead, gp_ahead, 0, ahead_sums)
         ahead_sums[h] = ahead_sums[h] * has_ahead
         send_ahead_sums(h).start()
@@ -202,14 +218,19 @@
             dq_give[h, half(i), :] = grad.astype(jnp.bfloat16)
             unit_q, _ = unit_rows(rq[h, half(i), :])
             gain_q += jnp.sum(grad * unit_q, axis=0, keepdims=True)
-        send_dq(h).start()
-        dk_acc[half(0), :] = dot(ds_low[half(0), half(0)], rqn[0, half(0), :])
-        dk_acc[half(1), :] = dot(ds_low[half(1), :], rqn[0])
-        dv_acc[half(0), :] = dot(p_low[half(0), half(0)], rg[h, half(0), :])
-        dv_acc[half(1), :] = dot(p_low[half(1), :], rg[h])
-
+        gain_part[h, pl.ds(0, 1), :] = gain_q
+        dk_acc[h, half(0), :] = dot(ds_low[half(0), half(0)], rqn[0, half(0), :])
+        dk_acc[h, half(1), :] = dot(ds_low[half(1), :], rqn[0])
+        dv_acc[h, half(0), :] = dot(p_low[half(0), half(0)], rg[h, half(0), :])
+        dv_acc[h, half(1), :] = dot(p_low[half(1), :], rg[h])
+
+    send_dq(1).start()
+
+    @pl.loop(0, HEADS)
+    def _(h):
         send_ahead_sums(h).wait_recv()
         probs_and_grads(h, OWN_BLOCKS, e_own, gp_own, h, own_sums, left_sums, None, p_low, ds_low)
+        gain_q = gain_part[h, pl.ds(0, 1), :]
         gain_k = jnp.zeros((1, HD), jnp.float32)
         for i in range(2):
             if i == 0:
@@ -220,8 +241,8 @@
                 dk = dot(ds_low[half(1), half(1)], qn[h, half(1), :])
                 dv = dot(p_low[half(1), half(1)], g[h, half(1), :])
                 dqt = dot(kt[h], ds_low[:, half(1)])
-            dv_o[h, half(i), :] = (dv + dv_acc[half(i), :]).astype(jnp.bfloat16)
-            grad_k = (dk + dk_acc[half(i), :]) * SCALE
+            dv_o[h, half(i), :] = (dv + dv_acc[h, half(i), :]).astype(jnp.bfloat16)
+            grad_k = (dk + dk_acc[h, half(i), :]) * SCALE
             unit_k, inv_k = unit_rows(k[h, half(i), :])
             gain_k += jnp.sum(grad_k * unit_k, axis=0, keepdims=True)
             dk_o[h, half(i), :] = norm_back(grad_k, unit_k, inv_k, gain_row(1, h))
@@ -234,10 +255,6 @@
         store(1, h).start()
         store(2, h).start()
 
-        @pl.when(h > 0)
-        def _():
-            finish_dq(h - 1)
-
     def head_of(d):
         return lax.div(d * width, HD)
 
@@ -259,6 +276,9 @@
     def _(i):
         send_dp(i).start()
 
+    send_dq(2).start()
+    send_dq(3).start()
+
     @pl.loop(1, n_dp)
     def _(i):
         send_dp(i).wait_recv()
@@ -272,7 +292,9 @@
     def _(i):
         send_ctx(i).start()
 
-    finish_dq(HEADS - 1)
+    @pl.loop(0, HEADS)
+    def _(h):
+        finish_dq(h)
 
     def from_ctx(i):
         at = lax.rem(me_c + n_ctx - i, n_ctx)
@@ -314,6 +336,15 @@
         send_ctx(i).wait_send()
 
 
+def hand_out(*refs):
+    sem = refs[8]
+    copies = [pltpu.make_async_copy(refs[i], refs[4 + i], sem.at[i]) for i in range(4)]
+    for copy in copies:
+        copy.start()
+    for copy in copies:
+        copy.wait()
+
+
 def per_device(n_dp, n_ctx, queries, keys, values, grad_out, gains):
     rows = queries.shape[1]
     low, wide = jnp.bfloat16, jnp.float32
@@ -322,12 +353,13 @@
     dma = pltpu.SemaphoreType.DMA
     any_space = pl.BlockSpec(memory_space=pl.ANY)
     vmem = pl.BlockSpec(memory_space=pltpu.VMEM)
-    big = jax.ShapeDtypeStruct(queries.shape, low)
-    return pl.pallas_call(
+    big = pltpu.VMEM(queries.shape, low)
+    hbm = pl.BlockSpec(memory_space=pltpu.HBM)
+    results = pl.pallas_call(
         functools.partial(kernel, n_dp, n_ctx),
-        out_shape=(big, big, big, jax.ShapeDtypeStruct((2, HEADS * HD // n_dp), wide)),
+        out_shape=(big, big, big, pltpu.VMEM((2, HEADS * HD // n_dp), wide)),
         in_specs=[any_space] * 4 + [vmem],
-        out_specs=(any_space, any_space, any_space, vmem),
+        out_specs=(vmem,) * 4,
         scratch_shapes=[heads_low] * 8
         + [
             pltpu.VMEM((HEADS, HD, rows), low),
@@ -338,8 +370,8 @@
             pltpu.VMEM((1, rows, rows), wide),
             pltpu.VMEM((rows, rows), low),
             pltpu.VMEM((rows, rows), low),
-            pltpu.VMEM((rows, HD), wide),
-            pltpu.VMEM((rows, HD), wide),
+            pltpu.VMEM((HEADS, rows, HD), wide),
+            pltpu.VMEM((HEADS, rows, HD), wide),
             pltpu.VMEM((HEADS, rows, HD), wide),
         ]
         + [heads_low] * 5
@@ -364,9 +396,17 @@
             dma((n_ctx,)),
         ],
         compiler_params=pltpu.CompilerParams(
-            collective_id=0, has_side_effects=True, vmem_limit_bytes=48 * 1024 * 1024
+            collective_id=0, has_side_effects=True, vmem_limit_bytes=60 * 1024 * 1024
         ),
     )(queries, keys, values, grad_out, gains)
+    return pl.pallas_call(
+        hand_out,
+        out_shape=tuple(jax.ShapeDtypeStruct(r.shape, r.dtype) for r in results),
+        in_specs=[any_space] * 4,
+        out_specs=(hbm,) * 4,
+        scratch_shapes=[dma((4,))],
+        compiler_params=pltpu.CompilerParams(vmem_limit_bytes=2 * 1024 * 1024),
+    )(*results)
 
 
 def solution(mesh):

time: 80.8 us -> 68.6 us (0.85)
  local copies, waits for them, and re-layouts: 7.79 us -> 0 us
  Pallas kernels: 72 us -> 67.8 us
    unnamed x14 -> x0, local copies, waits for them, and re-layouts: 7.79 us -> none
    pallas_call x1, Pallas kernels: 72 us -> 66.6 us  [per_device(): pl.pallas_call(functools.partial(kernel, n_dp, n_ctx), out_shape=(big, bi...]
    pallas_call x0 -> x1, Pallas kernels: none -> 1.18 us  [per_device(): pl.pallas_call(hand_out, out_shape=tuple((jax.ShapeDtypeStruct(r.shape, r...]
where the time goes in v2:
time: 68.6 us; the launch traced here: 68.4 us
  Pallas kernels  67.8 us (99%)
    pallas_call x1, Pallas kernels, per_device(): pl.pallas_call(functools.partial(kernel, n_dp, n_ctx), out_shape=(big, bi...  66.6 us

profile of v2, /device:TPU:1, one launch (start us, length us, event | category | flops | bytes accessed | tf_op | source)
XLA Modules:
  0.0 68.4 jit_solution(12510787176419861758)
XLA Ops:
  0.6 66.6 %shard_map.84 = (bf16[1,512,512]{2,1,0:T(8,128)(2,1)S(1)}, bf16[1,512,512]{2,1,0:T(8,128)(2,1)S(1)}, bf16[1,512,512]{2,1,0:T(8,128)(2,1)S(1)}, f32[2,32]{1,0:T(2,128)S(1)}) custom-call(bf16[1,512,512]{2,1,0:T(8,128)(2,1)} %q_hbm.1, bf16[1,512,512]{2,1,0:T(8,128)(2,1)} %k_hbm.1, bf16[1,512,512]{2,1,0:T(8,128)(2,1)} %v_hbm.1, bf16[1,512,512]{2,1,0:T(8,128)(2,1)} %g_hbm.1, ...), custom_call_target="tpu_custom_call" | custom-call | tf_op jit(solution)/shard_map/pallas_call | solution.py:358
  67.3 1.2 %shard_map.85 = (bf16[1,512,512]{2,1,0:T(8,128)(2,1)}, bf16[1,512,512]{2,1,0:T(8,128)(2,1)}, bf16[1,512,512]{2,1,0:T(8,128)(2,1)}, f32[2,32]{1,0:T(2,128)}) custom-call(bf16[1,512,512]{2,1,0:T(8,128)(2,1)S(1)} %get-tuple-element.8.refs_0_, bf16[1,512,512]{2,1,0:T(8,128)(2,1)S(1)} %get-tuple-element.9.refs_1_, ...), custom_call_target="tpu_custom_call" | custom-call | tf_op jit(solution)/shard_map/pallas_call | solution.py:402

commit v3 on v2

--- a/solution.py
+++ b/solution.py
@@ -12,6 +12,7 @@
 HD = 128
 EPS = 1e-06
 HALF = 256
+Z_HI, Z_LO = 2, 4
 SCALE = 1.0 / math.sqrt(HD)
 EXP2_SCALE = SCALE * math.log2(math.e)
 MESH = pl.DeviceIdType.MESH
@@ -91,9 +92,9 @@
     e_own, gp_own, e_ahead, gp_ahead, p_low, ds_low,
     dk_acc, dv_acc, dq_own, dq_give, dq_take, dq_o, dk_o, dv_o,
     own_sums, right_sums, ahead_sums, left_sums,
-    gain_part, dp_terms, ctx_terms,
+    gain_part, gain_terms,
     load_sem, fwd_send, fwd_recv, own_send, own_recv, ahead_send, ahead_recv,
-    dq_send, dq_recv, out_sem, dp_send, dp_recv, ctx_send, ctx_recv,
+    dq_send, dq_recv, out_sem, gain_send, gain_recv,
 ):
     me_d, me_c = lax.axis_index("dp"), lax.axis_index("ctx")
     left, right = lax.rem(me_c + n_ctx - 1, n_ctx), lax.rem(me_c + 1, n_ctx)
@@ -112,15 +113,30 @@
 
     barrier = pltpu.get_barrier_semaphore()
 
-    @pl.loop(1, n_dp)
-    def _(i):
-        pl.semaphore_signal(barrier, inc=1, device_id={"dp": lax.rem(me_d + i, n_dp)}, device_id_type=MESH)
-
-    @pl.loop(1, n_ctx)
-    def _(i):
-        pl.semaphore_signal(barrier, inc=1, device_id={"ctx": lax.rem(me_c + i, n_ctx)}, device_id_type=MESH)
-
-    pl.semaphore_wait(barrier, n_dp + n_ctx - 2)
+    n_in, n_y, n_z = n_dp // Z_HI, n_ctx // Z_LO, Z_HI * Z_LO
+    me_in, me_y = lax.rem(me_d, n_in), lax.div(me_c, Z_LO)
+    me_z = lax.div(me_d, n_in) * Z_LO + lax.rem(me_c, Z_LO)
+
+    def device(axis, at):
+        if axis == 0:
+            return {"dp": me_d - me_in + at}
+        if axis == 1:
+            return {"ctx": lax.rem(me_c, Z_LO) + at * Z_LO}
+        return {"dp": lax.div(at, Z_LO) * n_in + me_in, "ctx": me_y * Z_LO + lax.rem(at, Z_LO)}
+
+    axes = ((n_in, me_in), (n_y, me_y), (n_z, me_z))
+
+    for axis, (count, me) in enumerate(axes):
+
+        @pl.loop(1, count)
+        def _(i, axis=axis, count=count, me=me):
+            pl.semaphore_signal(
+                barrier, inc=1, device_id=device(axis, lax.rem(me + i, count)), device_id_type=MESH
+            )
+
+    for neighbour in (left, right):
+        pl.semaphore_signal(barrier, inc=1, device_id={"ctx": neighbour}, device_id_type=MESH)
+    pl.semaphore_wait(barrier, n_in + n_y + n_z - 1)
 
     def to_left(src, dst, send, recv):
         return pltpu.make_async_remote_copy(src, dst, send, recv, device_id={"ctx": left}, device_id_type=MESH)
@@ -199,13 +215,15 @@
             rqn[0, half(i), :] = (unit_q * gain_row(0, h)).astype(jnp.bfloat16)
         send_g(h).wait_recv()
 
-        @pl.when(h == HEADS - 1)
-        def _():
-            send_dq(0).start()
-
         exps_and_sums(h, AHEAD_BLOCKS, False, kn, v, rqn, rg, 0, e_ahead, gp_ahead, 0, ahead_sums)
         ahead_sums[h] = ahead_sums[h] * has_ahead
         send_ahead_sums(h).start()
+
+        @pl.when(h == HEADS - 1)
+        def _():
+            for earlier in range(HEADS - 1):
+                send_dq(earlier).start()
+
         send_own_sums(h).wait_recv()
         probs_and_grads(h, AHEAD_BLOCKS, e_ahead, gp_ahead, 0, right_sums, ahead_sums, has_ahead, p_low, ds_low)
         gain_q = jnp.zeros((1, HD), jnp.float32)
@@ -218,19 +236,22 @@
             dq_give[h, half(i), :] = grad.astype(jnp.bfloat16)
             unit_q, _ = unit_rows(rq[h, half(i), :])
             gain_q += jnp.sum(grad * unit_q, axis=0, keepdims=True)
-        gain_part[h, pl.ds(0, 1), :] = gain_q
+
+        @pl.when(h == HEADS - 1)
+        def _():
+            send_dq(HEADS - 1).start()
+
+        gain_part[0, h, pl.ds(0, 1), :] = gain_q
         dk_acc[h, half(0), :] = dot(ds_low[half(0), half(0)], rqn[0, half(0), :])
         dk_acc[h, half(1), :] = dot(ds_low[half(1), :], rqn[0])
         dv_acc[h, half(0), :] = dot(p_low[half(0), half(0)], rg[h, half(0), :])
         dv_acc[h, half(1), :] = dot(p_low[half(1), :], rg[h])
 
-    send_dq(1).start()
-
     @pl.loop(0, HEADS)
     def _(h):
         send_ahead_sums(h).wait_recv()
         probs_and_grads(h, OWN_BLOCKS, e_own, gp_own, h, own_sums, left_sums, None, p_low, ds_low)
-        gain_q = gain_part[h, pl.ds(0, 1), :]
+        gain_q = gain_part[0, h, pl.ds(0, 1), :]
         gain_k = jnp.zeros((1, HD), jnp.float32)
         for i in range(2):
             if i == 0:
@@ -250,72 +271,58 @@
             unit_q, _ = unit_rows(q[h, half(i), :])
             gain_q += jnp.sum(grad_q * unit_q, axis=0, keepdims=True)
             dq_own[h, half(i), :] = grad_q
-        gain_part[h, pl.ds(0, 1), :] = gain_q
-        gain_part[h, pl.ds(1, 1), :] = gain_k
+        gain_part[0, h, pl.ds(0, 1), :] = gain_q
+        gain_part[0, h, pl.ds(1, 1), :] = gain_k
         store(1, h).start()
         store(2, h).start()
 
-    def head_of(d):
-        return lax.div(d * width, HD)
-
-    def send_dp(i):
-        to = lax.rem(me_d + i, n_dp)
+    def send_gain(axis, i):
+        count, me = axes[axis]
         return pltpu.make_async_remote_copy(
-            gain_part.at[head_of(to)], dp_terms.at[i], dp_send.at[i], dp_recv.at[i],
-            device_id={"dp": to}, device_id_type=MESH,
+            gain_part.at[axis], gain_terms.at[axis, me], gain_send.at[axis, i], gain_recv.at[axis, i],
+            device_id=device(axis, lax.rem(me + i, count)), device_id_type=MESH,
         )
 
-    def send_ctx(i):
-        to = lax.rem(me_c + i, n_ctx)
-        return pltpu.make_async_remote_copy(
-            ctx_terms.at[me_c], ctx_terms.at[me_c], ctx_send.at[i], ctx_recv.at[i],
-            device_id={"ctx": to}, device_id_type=MESH,
-        )
-
-    @pl.loop(1, n_dp)
-    def _(i):
-        send_dp(i).start()
-
-    send_dq(2).start()
-    send_dq(3).start()
-
-    @pl.loop(1, n_dp)
-    def _(i):
-        send_dp(i).wait_recv()
-
-    term = gain_part[head_of(me_d)]
-    for i in range(1, n_dp):
-        term = term + dp_terms[i]
-    ctx_terms[me_c] = term
-
-    @pl.loop(1, n_ctx)
-    def _(i):
-        send_ctx(i).start()
+    def start_gains(axis):
+        @pl.loop(1, axes[axis][0])
+        def _(i):
+            send_gain(axis, i).start()
+
+    def sum_gains(axis):
+        count, me = axes[axis]
+        gain_terms[axis, me] = gain_part[axis]
+
+        @pl.loop(1, count)
+        def _(i):
+            at = gain_terms.at[axis, lax.rem(me + count - i, count)]
+            pltpu.make_async_remote_copy(
+                at, at, gain_send.at[axis, i], gain_recv.at[axis, i],
+                device_id=device(axis, lax.rem(me + i, count)), device_id_type=MESH,
+            ).wait_recv()
+
+        total = gain_terms[axis, 0]
+        for i in range(1, count):
+            total = total + gain_terms[axis, i]
+        gain_part[axis + 1] = total
+
+    start_gains(0)
+    sum_gains(0)
+    start_gains(1)
+    sum_gains(1)
+    start_gains(2)
 
     @pl.loop(0, HEADS)
     def _(h):
         finish_dq(h)
 
-    def from_ctx(i):
-        at = lax.rem(me_c + n_ctx - i, n_ctx)
-        return pltpu.make_async_remote_copy(
-            ctx_terms.at[at], ctx_terms.at[at], ctx_send.at[i], ctx_recv.at[i],
-            device_id={"ctx": lax.rem(me_c + i, n_ctx)}, device_id_type=MESH,
-        )
-
-    @pl.loop(1, n_ctx)
-    def _(i):
-        from_ctx(i).wait_recv()
-
-    total = ctx_terms[0]
-    for i in range(1, n_ctx):
-        total = total + ctx_terms[i]
+    sum_gains(2)
     per_head = HD // width
+    mine = gain_part[3, lax.div(me_d, per_head)]
     for j in range(per_head):
 
         @pl.when(lax.rem(me_d, per_head) == j)
         def _(j=j):
-            gain_out[...] = total[:, j * width : (j + 1) * width]
+            gain_out[...] = mine[:, j * width : (j + 1) * width]
 
     @pl.loop(0, HEADS)
     def _(h):
@@ -327,13 +334,11 @@
         for a in range(3):
             store(a, h).wait()
 
-    @pl.loop(1, n_dp)
-    def _(i):
-        send_dp(i).wait_send()
-
-    @pl.loop(1, n_ctx)
-    def _(i):
-        send_ctx(i).wait_send()
+    for axis in range(3):
+
+        @pl.loop(1, axes[axis][0])
+        def _(i, axis=axis):
+            send_gain(axis, i).wait_send()
 
 
 def hand_out(*refs):
@@ -347,6 +352,7 @@
 
 def per_device(n_dp, n_ctx, queries, keys, values, grad_out, gains):
     rows = queries.shape[1]
+    most = max(n_dp // Z_HI, n_ctx // Z_LO, Z_HI * Z_LO)
     low, wide = jnp.bfloat16, jnp.float32
     heads_low = pltpu.VMEM((HEADS, rows, HD), low)
     sums = pltpu.VMEM((HEADS, 8, HD), wide)
@@ -377,9 +383,8 @@
         + [heads_low] * 5
         + [sums] * 4
         + [
-            pltpu.VMEM((HEADS, 2, HD), wide),
-            pltpu.VMEM((n_dp, 2, HD), wide),
-            pltpu.VMEM((n_ctx, 2, HD), wide),
+            pltpu.VMEM((4, HEADS, 2, HD), wide),
+            pltpu.VMEM((3, most, HEADS, 2, HD), wide),
             dma((4, HEADS)),
             dma((2, HEADS)),
             dma((2, HEADS)),
@@ -390,10 +395,8 @@
             dma((HEADS,)),
             dma((HEADS,)),
             dma((3, HEADS)),
-            dma((n_dp,)),
-            dma((n_dp,)),
-            dma((n_ctx,)),
-            dma((n_ctx,)),
+            dma((3, most)),
+            dma((3, most)),
         ],
         compiler_params=pltpu.CompilerParams(
             collective_id=0, has_side_effects=True, vmem_limit_bytes=60 * 1024 * 1024

time: 68.6 us -> 63.2 us (0.921)
  Pallas kernels: 67.8 us -> 62.4 us
    pallas_call x1, Pallas kernels: 66.6 us -> 61.2 us  [per_device(): pl.pallas_call(functools.partial(kernel, n_dp, n_ctx), out_shape=(big, bi...]
where the time goes in v3:
time: 63.2 us; the launch traced here: 63.1 us
  Pallas kernels  62.4 us (99%)
  between operations  0.64 us (1%)
    pallas_call x1, Pallas kernels, per_device(): pl.pallas_call(functools.partial(kernel, n_dp, n_ctx), out_shape=(big, bi...  61.2 us

profile of v3, /device:TPU:1, one launch (start us, length us, event | category | flops | bytes accessed | tf_op | source)
XLA Modules:
  0.0 63.1 jit_solution(1108620916098500671)
XLA Ops:
  0.6 61.2 %shard_map.84 = (bf16[1,512,512]{2,1,0:T(8,128)(2,1)S(1)}, bf16[1,512,512]{2,1,0:T(8,128)(2,1)S(1)}, bf16[1,512,512]{2,1,0:T(8,128)(2,1)S(1)}, f32[2,32]{1,0:T(2,128)S(1)}) custom-call(bf16[1,512,512]{2,1,0:T(8,128)(2,1)} %q_hbm.1, bf16[1,512,512]{2,1,0:T(8,128)(2,1)} %k_hbm.1, bf16[1,512,512]{2,1,0:T(8,128)(2,1)} %v_hbm.1, bf16[1,512,512]{2,1,0:T(8,128)(2,1)} %g_hbm.1, ...), custom_call_target="tpu_custom_call" | custom-call | tf_op jit(solution)/shard_map/pallas_call | solution.py:364
  61.9 1.2 %shard_map.85 = (bf16[1,512,512]{2,1,0:T(8,128)(2,1)}, bf16[1,512,512]{2,1,0:T(8,128)(2,1)}, bf16[1,512,512]{2,1,0:T(8,128)(2,1)}, f32[2,32]{1,0:T(2,128)}) custom-call(bf16[1,512,512]{2,1,0:T(8,128)(2,1)S(1)} %get-tuple-element.8.refs_0_, bf16[1,512,512]{2,1,0:T(8,128)(2,1)S(1)} %get-tuple-element.9.refs_1_, ...), custom_call_target="tpu_custom_call" | custom-call | tf_op jit(solution)/shard_map/pallas_call | solution.py:405

commit v4 on v3

--- a/solution.py
+++ b/solution.py
@@ -12,6 +12,7 @@
 HD = 128
 EPS = 1e-06
 HALF = 256
+LAST = HEADS - 1
 Z_HI, Z_LO = 2, 4
 SCALE = 1.0 / math.sqrt(HD)
 EXP2_SCALE = SCALE * math.log2(math.e)
@@ -45,11 +46,11 @@
     return (inverse * (scaled - unit * mean_term)).astype(jnp.bfloat16)
 
 
-def exps_and_sums(h, blocks, own, kn, v, qn, g, qh, e, gp, eh, sums):
+def exps_and_sums(h, blocks, own, kn, kh, v, qn, qh, g, e, gp, eh, sums):
     total = [None, None]
     weighted = [None, None]
     for kb, qb, edge in blocks:
-        s = dot_nt(kn[h, half(kb), :], qn[qh, half(qb), :])
+        s = dot_nt(kn[kh, half(kb), :], qn[qh, half(qb), :])
         ex = jnp.exp2(s * EXP2_SCALE)
         if edge:
             key = lax.broadcasted_iota(jnp.int32, (HALF, HALF), 0)
@@ -100,6 +101,7 @@
     left, right = lax.rem(me_c + n_ctx - 1, n_ctx), lax.rem(me_c + 1, n_ctx)
     width = HEADS * HD // n_dp
     has_ahead = jnp.where(me_c < n_ctx - 1, 1.0, 0.0).astype(jnp.float32)
+    has_behind = jnp.where(me_c > 0, 1.0, 0.0).astype(jnp.float32)
 
     loads = ((q_hbm, q), (g_hbm, g), (k_hbm, k), (v_hbm, v))
 
@@ -158,6 +160,16 @@
 
     def send_dq(h):
         return to_right(dq_give.at[h], dq_take.at[h], dq_send.at[h], dq_recv.at[h])
+
+    def send_k():
+        return to_right(k.at[LAST], rq.at[LAST], fwd_send.at[0, LAST], fwd_recv.at[0, LAST])
+
+    def send_v():
+        return to_right(v.at[LAST], rg.at[LAST], fwd_send.at[1, LAST], fwd_recv.at[1, LAST])
+
+    def send_back(j):
+        at = LAST + j
+        return to_left(dq_give.at[at], dq_take.at[at], dq_send.at[at], dq_recv.at[at])
 
     def store(a, h):
         src, dst = ((dq_o, dq_hbm), (dk_o, dk_hbm), (dv_o, dv_hbm))[a]
@@ -189,15 +201,17 @@
             normed = unit_k * gain_row(1, h)
             kn[h, half(i), :] = normed.astype(jnp.bfloat16)
             kt[h, :, half(i)] = normed.T.astype(jnp.bfloat16)
-        exps_and_sums(h, OWN_BLOCKS, True, kn, v, qn, g, h, e_own, gp_own, h, own_sums)
-        send_own_sums(h).start()
+        exps_and_sums(h, OWN_BLOCKS, True, kn, h, v, qn, h, g, e_own, gp_own, h, own_sums)
+
+        @pl.when(h < LAST)
+        def _():
+            send_own_sums(h).start()
 
         @pl.when(h == 1)
         def _():
             send_ahead(1)
 
     send_ahead(2)
-    send_ahead(3)
 
     def finish_dq(h):
         send_dq(h).wait_recv()
@@ -207,22 +221,23 @@
             dq_o[h, half(i), :] = norm_back(grad, unit_q, inv_q, gain_row(0, h))
         store(0, h).start()
 
-    @pl.loop(0, HEADS)
+    @pl.loop(0, LAST)
     def _(h):
         send_q(h).wait_recv()
         for i in range(2):
             unit_q, _ = unit_rows(rq[h, half(i), :])
             rqn[0, half(i), :] = (unit_q * gain_row(0, h)).astype(jnp.bfloat16)
+
+        @pl.when(h == LAST - 1)
+        def _():
+            send_k().start()
+            send_v().start()
+
         send_g(h).wait_recv()
 
-        exps_and_sums(h, AHEAD_BLOCKS, False, kn, v, rqn, rg, 0, e_ahead, gp_ahead, 0, ahead_sums)
+        exps_and_sums(h, AHEAD_BLOCKS, False, kn, h, v, rqn, 0, rg, e_ahead, gp_ahead, 0, ahead_sums)
         ahead_sums[h] = ahead_sums[h] * has_ahead
         send_ahead_sums(h).start()
-
-        @pl.when(h == HEADS - 1)
-        def _():
-            for earlier in range(HEADS - 1):
-                send_dq(earlier).start()
 
         send_own_sums(h).wait_recv()
         probs_and_grads(h, AHEAD_BLOCKS, e_ahead, gp_ahead, 0, right_sums, ahead_sums, has_ahead, p_low, ds_low)
@@ -236,19 +251,13 @@
             dq_give[h, half(i), :] = grad.astype(jnp.bfloat16)
             unit_q, _ = unit_rows(rq[h, half(i), :])
             gain_q += jnp.sum(grad * unit_q, axis=0, keepdims=True)
-
-        @pl.when(h == HEADS - 1)
-        def _():
-            send_dq(HEADS - 1).start()
-
         gain_part[0, h, pl.ds(0, 1), :] = gain_q
         dk_acc[h, half(0), :] = dot(ds_low[half(0), half(0)], rqn[0, half(0), :])
         dk_acc[h, half(1), :] = dot(ds_low[half(1), :], rqn[0])
         dv_acc[h, half(0), :] = dot(p_low[half(0), half(0)], rg[h, half(0), :])
         dv_acc[h, half(1), :] = dot(p_low[half(1), :], rg[h])
 
-    @pl.loop(0, HEADS)
-    def _(h):
+    def own_part(h):
         send_ahead_sums(h).wait_recv()
         probs_and_grads(h, OWN_BLOCKS, e_own, gp_own, h, own_sums, left_sums, None, p_low, ds_low)
         gain_q = gain_part[0, h, pl.ds(0, 1), :]
@@ -276,6 +285,83 @@
         store(1, h).start()
         store(2, h).start()
 
+    def last_part():
+        h = LAST
+        send_k().wait_recv()
+        for i in range(2):
+            unit_k, _ = unit_rows(rq[h, half(i), :])
+            normed = unit_k * gain_row(1, h)
+            rqn[0, half(i), :] = normed.astype(jnp.bfloat16)
+            kt[HEADS, :, half(i)] = normed.T.astype(jnp.bfloat16)
+        send_v().wait_recv()
+        for earlier in range(LAST):
+            send_dq(earlier).start()
+        exps_and_sums(h, AHEAD_BLOCKS, False, rqn, 0, rg, qn, h, g, e_ahead, gp_ahead, 0, ahead_sums)
+        ahead_sums[h] = ahead_sums[h] * has_behind
+        probs_and_grads(h, AHEAD_BLOCKS, e_ahead, gp_ahead, 0, own_sums, ahead_sums, has_behind, p_low, ds_low)
+        gain_q = jnp.zeros((1, HD), jnp.float32)
+        gain_k = jnp.zeros((1, HD), jnp.float32)
+        for i in range(2):
+            if i == 0:
+                dk = dot(ds_low[half(0), half(0)], qn[h, half(0), :])
+                dv = dot(p_low[half(0), half(0)], g[h, half(0), :])
+                dqt = dot(kt[HEADS], ds_low[:, half(0)])
+            else:
+                dk = dot(ds_low[half(1), :], qn[h])
+                dv = dot(p_low[half(1), :], g[h])
+                dqt = dot(kt[HEADS, :, half(1)], ds_low[half(1), half(1)])
+            grad_k = dk * SCALE
+            unit_k, _ = unit_rows(rq[h, half(i), :])
+            gain_k += jnp.sum(grad_k * unit_k, axis=0, keepdims=True)
+            dq_give[h, half(i), :] = grad_k.astype(jnp.bfloat16)
+            dq_give[h + 1, half(i), :] = dv.astype(jnp.bfloat16)
+            dq_own[h, half(i), :] = dqt.T * SCALE
+        send_back(0).start()
+        send_back(1).start()
+        probs_and_grads(h, OWN_BLOCKS, e_own, gp_own, h, own_sums, ahead_sums, None, p_low, ds_low)
+        for i in range(2):
+            if i == 0:
+                dk = dot(ds_low[half(0), :], qn[h])
+                dv = dot(p_low[half(0), :], g[h])
+                dqt = dot(kt[h, :, half(0)], ds_low[half(0), half(0)])
+            else:
+                dk = dot(ds_low[half(1), half(1)], qn[h, half(1), :])
+                dv = dot(p_low[half(1), half(1)], g[h, half(1), :])
+                dqt = dot(kt[h], ds_low[:, half(1)])
+            dv_acc[h, half(i), :] = dv
+            grad_k = dk * SCALE
+            dk_acc[h, half(i), :] = grad_k
+            unit_k, _ = unit_rows(k[h, half(i), :])
+            gain_k += jnp.sum(grad_k * unit_k, axis=0, keepdims=True)
+            grad_q = dq_own[h, half(i), :] + dqt.T * SCALE
+            unit_q, inv_q = unit_rows(q[h, half(i), :])
+            gain_q += jnp.sum(grad_q * unit_q, axis=0, keepdims=True)
+            dq_o[h, half(i), :] = norm_back(grad_q, unit_q, inv_q, gain_row(0, h))
+        gain_part[0, h, pl.ds(0, 1), :] = gain_q
+        gain_part[0, h, pl.ds(1, 1), :] = gain_k
+        store(0, h).start()
+
+    def finish_last():
+        h = LAST
+        send_back(0).wait_recv()
+        send_back(1).wait_recv()
+        for i in range(2):
+            grad_k = dk_acc[h, half(i), :] + dq_take[h, half(i), :].astype(jnp.float32)
+            unit_k, inv_k = unit_rows(k[h, half(i), :])
+            dk_o[h, half(i), :] = norm_back(grad_k, unit_k, inv_k, gain_row(1, h))
+            dv = dv_acc[h, half(i), :] + dq_take[h + 1, half(i), :].astype(jnp.float32)
+            dv_o[h, half(i), :] = dv.astype(jnp.bfloat16)
+        store(1, h).start()
+        store(2, h).start()
+
+    @pl.loop(0, LAST)
+    def _(h):
+        @pl.when(h == LAST - 1)
+        def _():
+            last_part()
+
+        own_part(h)
+
     def send_gain(axis, i):
         count, me = axes[axis]
         return pltpu.make_async_remote_copy(
@@ -311,9 +397,11 @@
     sum_gains(1)
     start_gains(2)
 
-    @pl.loop(0, HEADS)
+    @pl.loop(0, LAST)
     def _(h):
         finish_dq(h)
+
+    finish_last()
 
     sum_gains(2)
     per_head = HD // width
@@ -324,13 +412,21 @@
         def _(j=j):
             gain_out[...] = mine[:, j * width : (j + 1) * width]
 
-    @pl.loop(0, HEADS)
+    @pl.loop(0, LAST)
     def _(h):
         send_q(h).wait_send()
         send_g(h).wait_send()
         send_own_sums(h).wait_send()
         send_ahead_sums(h).wait_send()
         send_dq(h).wait_send()
+
+    send_k().wait_send()
+    send_v().wait_send()
+    send_back(0).wait_send()
+    send_back(1).wait_send()
+
+    @pl.loop(0, HEADS)
+    def _(h):
         for a in range(3):
             store(a, h).wait()
 
@@ -368,7 +464,7 @@
         out_specs=(vmem,) * 4,
         scratch_shapes=[heads_low] * 8
         + [
-            pltpu.VMEM((HEADS, HD, rows), low),
+            pltpu.VMEM((HEADS + 1, HD, rows), low),
             pltpu.VMEM((1, rows, HD), low),
             pltpu.VMEM((HEADS, rows, rows), wide),
             pltpu.VMEM((HEADS, rows, rows), wide),
@@ -380,7 +476,8 @@
             pltpu.VMEM((HEADS, rows, HD), wide),
             pltpu.VMEM((HEADS, rows, HD), wide),
         ]
-        + [heads_low] * 5
+        + [pltpu.VMEM((HEADS + 1, rows, HD), low)] * 2
+        + [heads_low] * 3
         + [sums] * 4
         + [
             pltpu.VMEM((4, HEADS, 2, HD), wide),
@@ -392,8 +489,8 @@
             dma((HEADS,)),
             dma((HEADS,)),
             dma((HEADS,)),
-            dma((HEADS,)),
-            dma((HEADS,)),
+            dma((HEADS + 1,)),
+            dma((HEADS + 1,)),
             dma((3, HEADS)),
             dma((3, most)),
             dma((3, most)),

time: 63.2 us -> 60 us (0.949)
  Pallas kernels: 62.4 us -> 59.2 us
    pallas_call x1, Pallas kernels: 61.2 us -> 58.1 us  [per_device(): pl.pallas_call(functools.partial(kernel, n_dp, n_ctx), out_shape=(big, bi...]
where the time goes in v4:
time: 60 us; the launch traced here: 59.9 us
  Pallas kernels  59.2 us (99%)
  between operations  0.64 us (1%)
    pallas_call x1, Pallas kernels, per_device(): pl.pallas_call(functools.partial(kernel, n_dp, n_ctx), out_shape=(big, bi...  58.1 us

profile of v4, /device:TPU:1, one launch (start us, length us, event | category | flops | bytes accessed | tf_op | source)
XLA Modules:
  0.0 59.9 jit_solution(4496488024512007456)
XLA Ops:
  0.6 58.1 %shard_map.84 = (bf16[1,512,512]{2,1,0:T(8,128)(2,1)S(1)}, bf16[1,512,512]{2,1,0:T(8,128)(2,1)S(1)}, bf16[1,512,512]{2,1,0:T(8,128)(2,1)S(1)}, f32[2,32]{1,0:T(2,128)S(1)}) custom-call(bf16[1,512,512]{2,1,0:T(8,128)(2,1)} %q_hbm.1, bf16[1,512,512]{2,1,0:T(8,128)(2,1)} %k_hbm.1, bf16[1,512,512]{2,1,0:T(8,128)(2,1)} %v_hbm.1, bf16[1,512,512]{2,1,0:T(8,128)(2,1)} %g_hbm.1, ...), custom_call_target="tpu_custom_call" | custom-call | tf_op jit(solution)/shard_map/pallas_call | solution.py:460
  58.7 1.2 %shard_map.85 = (bf16[1,512,512]{2,1,0:T(8,128)(2,1)}, bf16[1,512,512]{2,1,0:T(8,128)(2,1)}, bf16[1,512,512]{2,1,0:T(8,128)(2,1)}, f32[2,32]{1,0:T(2,128)}) custom-call(bf16[1,512,512]{2,1,0:T(8,128)(2,1)S(1)} %get-tuple-element.8.refs_0_, bf16[1,512,512]{2,1,0:T(8,128)(2,1)S(1)} %get-tuple-element.9.refs_1_, ...), custom_call_target="tpu_custom_call" | custom-call | tf_op jit(solution)/shard_map/pallas_call | solution.py:502

commit v5 on v4

--- a/solution.py
+++ b/solution.py
@@ -334,15 +334,18 @@
             unit_k, _ = unit_rows(k[h, half(i), :])
             gain_k += jnp.sum(grad_k * unit_k, axis=0, keepdims=True)
             grad_q = dq_own[h, half(i), :] + dqt.T * SCALE
-            unit_q, inv_q = unit_rows(q[h, half(i), :])
+            unit_q, _ = unit_rows(q[h, half(i), :])
             gain_q += jnp.sum(grad_q * unit_q, axis=0, keepdims=True)
-            dq_o[h, half(i), :] = norm_back(grad_q, unit_q, inv_q, gain_row(0, h))
+            dq_own[h, half(i), :] = grad_q
         gain_part[0, h, pl.ds(0, 1), :] = gain_q
         gain_part[0, h, pl.ds(1, 1), :] = gain_k
-        store(0, h).start()
 
     def finish_last():
         h = LAST
+        for i in range(2):
+            unit_q, inv_q = unit_rows(q[h, half(i), :])
+            dq_o[h, half(i), :] = norm_back(dq_own[h, half(i), :], unit_q, inv_q, gain_row(0, h))
+        store(0, h).start()
         send_back(0).wait_recv()
         send_back(1).wait_recv()
         for i in range(2):
@@ -370,8 +373,8 @@
         )
 
     def start_gains(axis):
-        @pl.loop(1, axes[axis][0])
-        def _(i):
+        count = axes[axis][0]
+        for i in sorted(range(1, count), key=lambda i: abs(i - count // 2)):
             send_gain(axis, i).start()
 
     def sum_gains(axis):

time: 60 us -> 59.7 us (level)
  no operation moved by 1% of the time
where the time goes in v5:
time: 59.7 us; the launch traced here: 59.4 us
  Pallas kernels  58.8 us (98%)
  between operations  0.64 us (1%)
    pallas_call x1, Pallas kernels, per_device(): pl.pallas_call(functools.partial(kernel, n_dp, n_ctx), out_shape=(big, bi...  57.6 us

profile of v5, /device:TPU:1, one launch (start us, length us, event | category | flops | bytes accessed | tf_op | source)
XLA Modules:
  0.0 59.4 jit_solution(9332365387522232825)
XLA Ops:
  0.6 57.6 %shard_map.84 = (bf16[1,512,512]{2,1,0:T(8,128)(2,1)S(1)}, bf16[1,512,512]{2,1,0:T(8,128)(2,1)S(1)}, bf16[1,512,512]{2,1,0:T(8,128)(2,1)S(1)}, f32[2,32]{1,0:T(2,128)S(1)}) custom-call(bf16[1,512,512]{2,1,0:T(8,128)(2,1)} %q_hbm.1, bf16[1,512,512]{2,1,0:T(8,128)(2,1)} %k_hbm.1, bf16[1,512,512]{2,1,0:T(8,128)(2,1)} %v_hbm.1, bf16[1,512,512]{2,1,0:T(8,128)(2,1)} %g_hbm.1, ...), custom_call_target="tpu_custom_call" | custom-call | tf_op jit(solution)/shard_map/pallas_call | solution.py:463
  58.2 1.2 %shard_map.85 = (bf16[1,512,512]{2,1,0:T(8,128)(2,1)}, bf16[1,512,512]{2,1,0:T(8,128)(2,1)}, bf16[1,512,512]{2,1,0:T(8,128)(2,1)}, f32[2,32]{1,0:T(2,128)}) custom-call(bf16[1,512,512]{2,1,0:T(8,128)(2,1)S(1)} %get-tuple-element.8.refs_0_, bf16[1,512,512]{2,1,0:T(8,128)(2,1)S(1)} %get-tuple-element.9.refs_1_, ...), custom_call_target="tpu_custom_call" | custom-call | tf_op jit(solution)/shard_map/pallas_call | solution.py:505
